TPU v7x, 32 devices: a whole 2x2x4 slice. The times are simulated.
32 devices in a mesh: ep: 16 (over z, x, core), tp: 2 (over y).
Axes of the slice: x: 2, y: 2, z: 4, core: 2. Of those that a mesh axis runs over, the one named last changes fastest.
Arguments:
- tokens: bfloat16 [256, 7168], P('ep', 'tp'), may hold values from -6 to 6
- expert_ids: int32 [256, 8], P('ep'), may hold values from 0 to 15, all different within a row; in each aligned block of 16 rows (0 to 15, 16 to 31, ...) at most 16 rows name the same one
- gate_weights: float32 [256, 8], P('ep'), may hold values from 0.05 to 0.6
- w_gate: bfloat16 [16, 7168, 2048], P('ep', None, 'tp'), may hold values from -0.0625 to 0.0625
- w_up: bfloat16 [16, 7168, 2048], P('ep', None, 'tp'), may hold values from -0.0625 to 0.0625
- w_down: bfloat16 [16, 2048, 7168], P('ep', None, 'tp'), may hold values from -0.125 to 0.125
Outputs:
- moe_out: bfloat16 [256, 7168], P('ep', 'tp')
Inputs may be any that keep to these rules, and one draw needn't show every extreme that they name: `expert_ids`: each row names 8 different experts. Among the 16 rows of one index of ep (aligned blocks) no expert is named by more than 16 rows, a bound that some block reaches.
All inputs are finite; a program needn't handle non-finite values.
Results may differ from a plain program's by a relative error of at most 0.012.
Values may be sent and summed in bfloat16 or wider, within the bound.
A program may use at most 128 MiB of HBM per device.

v0:
```python
import jax
import jax.numpy as jnp
from jax import lax
from jax.sharding import PartitionSpec as P

CAP = 16


def slot_index(group_ids, n_experts, slots):
    flat_ids = group_ids.reshape(-1)
    onehot = (flat_ids[:, None] == jnp.arange(n_experts, dtype=jnp.int32)[None, :]).astype(
        jnp.int32
    )
    before = jnp.cumsum(onehot, axis=0) - onehot
    position = jnp.sum(before * onehot, axis=1)
    return flat_ids * slots + position


def per_device(tokens, expert_ids, gate_weights, w_gate, w_up, w_down):
    n_experts = lax.axis_size("ep")
    group_len = expert_ids.shape[0]
    choose = expert_ids.shape[1]
    slot_of = slot_index(expert_ids, n_experts, CAP)
    source = lax.all_gather(tokens, "tp", axis=1, tiled=True)
    slot_ids = jnp.arange(n_experts * CAP, dtype=jnp.int32)
    chooser = jnp.any(
        slot_of.reshape(group_len, choose)[None, :, :] == slot_ids[:, None, None], axis=2
    ).astype(jnp.bfloat16)
    outbound = jnp.dot(chooser, source, preferred_element_type=jnp.float32).astype(jnp.bfloat16)
    outbound = outbound.reshape(n_experts, CAP, source.shape[1])
    gate_local = w_gate[0]
    up_local = w_up[0]
    down_local = w_down[0]
    received = lax.all_to_all(outbound, "ep", split_axis=0, concat_axis=0, tiled=True)
    columns = received.shape[2]
    slot_count = received.shape[1]
    in_rows = received.reshape(-1, columns)
    gate_sum = jnp.dot(in_rows, gate_local, preferred_element_type=jnp.float32)
    up_sum = jnp.dot(in_rows, up_local, preferred_element_type=jnp.float32)
    hidden = (jax.nn.silu(gate_sum) * up_sum).astype(jnp.bfloat16)
    result = jnp.dot(
        lax.all_gather(hidden, "tp", axis=1, tiled=True),
        down_local,
        preferred_element_type=jnp.float32,
    ).astype(jnp.bfloat16)
    result = result.reshape(received.shape[0], slot_count, down_local.shape[1])
    returned = lax.all_to_all(result, "ep", split_axis=0, concat_axis=0, tiled=True)
    returned_rows = returned.reshape(-1, returned.shape[2])
    picked = returned_rows[slot_of].reshape(group_len, choose, returned_rows.shape[1])
    mixed = jnp.einsum("gk,gkd->gd", gate_weights, picked.astype(jnp.float32))
    return mixed.astype(jnp.bfloat16)


def solution(mesh):
    return jax.shard_map(
        per_device,
        mesh=mesh,
        in_specs=(
            P("ep", "tp"),
            P("ep", None),
            P("ep", None),
            P("ep", None, "tp"),
            P("ep", None, "tp"),
            P("ep", None, "tp"),
        ),
        out_specs=P("ep", "tp"),
        check_vma=False,
    )
```

profile of v0, /device:TPU:11, one launch (start us, length us, event | category | flops | bytes accessed | tf_op | source)
XLA Modules:
  0.0 205.0 jit_solution(89638607948516761)
XLA Ops:
  6.5 0.0 all-gather.2.cloned.1.call-start
  6.5 0.8 copy.11
  7.3 0.1 eq.28
  7.4 0.1 fusion.18
  7.5 0.2 reduce_window_sum.11
  7.7 0.2 select_reduce_fusion
  7.8 0.1 reduce_sum.14
  7.9 0.1 fusion.17
  8.1 4.9 %all_gather.6 = bf16[16,7168]{1,0:T(8,128)(2,1)S(1)} all-gather(bf16[16,3584]{1,0:T(8,128)(2,1)} %param.6), channel_id=1, replica_groups=mesh['ep'=16,'tp'=2] {'tp'}, dimensions={1}, use_global_device_ids=true | all-gather | bytes 344064 | tf_op jit(solution)/shard_map/all_gather | solution.py:24
  13.0 1.1 convolution_convert_fusion
  14.1 0.0 slice-start
  14.1 88.5 %all_to_all.10 = bf16[16,16,7168]{2,1,0:T(8,128)(2,1)S(1)} all-to-all(bf16[16,16,7168]{2,1,0:T(8,128)(2,1)S(1)} %bitcast.39), channel_id=1, replica_groups=mesh['ep'=16,'tp'=2] {'ep'}, dimensions={0} | all-to-all | bytes 7340032 | tf_op jit(solution)/shard_map/all_to_all | solution.py:34
  102.6 0.0 slice-start.1
  102.6 0.0 slice-start.2
  102.6 0.0 slice-start.3
  102.6 7.4 %fusion.4 = f32[256,1024]{1,0:T(8,128)S(1)} fusion(bf16[256,7168]{1,0:T(8,128)(2,1)S(1)} %bitcast.40, bf16[1,7168,1024]{2,1,0:T(8,128)(2,1)} %param.9), kind=kOutput, calls=%fused_computation.5 | convolution fusion | flops 3758096384 | bytes 19398656 | tf_op jit(solution)/shard_map/dot_general | solution.py:38
  110.0 0.0 slice-done
  110.0 0.0 slice-done.1
  110.1 0.2 slice-done.2
  110.3 0.6 slice-done.3
  110.9 4.8 %fusion.12 = bf16[256,1024]{1,0:T(8,128)(2,1)} fusion(bf16[256,7168]{1,0:T(8,128)(2,1)S(1)} %bitcast.41, bf16[1,7168,1024]{2,1,0:T(8,128)(2,1)S(1)} %bitcast.45, f32[256,1024]{1,0:T(8,128)S(1)} %fusion.4), kind=kOutput, calls=%fused_computation.10 | convolution fusion | flops 3759669248 | bytes 19922944 | tf_op jit(solution)/shard_map/dot_general | solution.py:39
  115.7 0.0 all-gather.2.cloned.1.call-update
  115.7 21.3 %all-gather.2.cloned.1.call-done = bf16[256,2048]{1,0:T(8,128)(2,1)} async-done(((bf16[256,1024]{1,0:T(8,128)(2,1)}), bf16[256,2048]{1,0:T(8,128)(2,1)}) %all-gather.2.cloned.1.call-update) | async-done | bytes 1048592 | tf_op jit(solution)/shard_map/all_gather | solution.py:42
  137.0 10.7 %fusion.6 = bf16[256,3584]{1,0:T(8,128)(2,1)} fusion(bf16[256,2048]{1,0:T(8,128)(2,1)} %all-gather.2.cloned.1.call-done, bf16[1,2048,3584]{2,1,0:T(8,128)(2,1)} %param.11), kind=kOutput, calls=%fused_computation.8 | convolution fusion | flops 3759013888 | bytes 17563648 | tf_op jit(solution)/shard_map/dot_general | solution.py:41
  147.7 0.0 copy-start
  147.7 6.5 %all-to-all-start.1 = ((bf16[16,16,3584]{2,1,0:T(8,128)(2,1)}), bf16[16,16,3584]{2,1,0:T(8,128)(2,1)S(1)}, u32[]{:S(2)}, u32[]{:S(2)}) async-start(bf16[16,16,3584]{2,1,0:T(8,128)(2,1)} %bitcast.42), calls=%async_computation.1 | async-start | bytes 3670016 | tf_op jit(solution)/shard_map/all_to_all | solution.py:47
  154.2 0.1 mul.33
  154.3 0.0 copy-done
  154.3 0.1 copy.13
  154.4 41.6 %all-to-all-done.1 = bf16[16,16,3584]{2,1,0:T(8,128)(2,1)S(1)} async-done(((bf16[16,16,3584]{2,1,0:T(8,128)(2,1)}), bf16[16,16,3584]{2,1,0:T(8,128)(2,1)S(1)}, u32[]{:S(2)}, u32[]{:S(2)}) %all-to-all-start.1) | async-done | bytes 1835040 | tf_op jit(solution)/shard_map/all_to_all | solution.py:47
  196.0 1.1 gather_fusion
  197.1 0.4 fusion.15
  197.5 0.7 copy.16
  (4 shorter events, 0.0 us)
Async XLA Ops:
  6.5 130.5 %all-gather.2.cloned.1.call-start = ((), (), s32[]{:S(2)}) async-start(), calls=%async_computation.2 | async-start | bytes 1572864 | tf_op jit(solution)/shard_map/all_gather | solution.py:42
  14.1 95.9 %slice-start = ((s8[14680064]{0:T(1024)(128)(4,1)}), s8[4194304]{0:T(1024)(128)(4,1)S(1)}, s32[]{:S(2)}) async-start(s8[14680064]{0:T(1024)(128)(4,1)} %bitcast.44), calls=%async_computation.3 | async-start | bytes 8388608
  102.6 7.4 %slice-start.1 = ((s8[14680064]{0:T(1024)(128)(4,1)}), s8[4194304]{0:T(1024)(128)(4,1)S(1)}, s32[]{:S(2)}) async-start(s8[14680064]{0:T(1024)(128)(4,1)} %bitcast.44), calls=%async_computation.4 | async-start | bytes 8388608
  102.6 7.6 %slice-start.2 = ((s8[14680064]{0:T(1024)(128)(4,1)}), s8[4194304]{0:T(1024)(128)(4,1)S(1)}, s32[]{:S(2)}) async-start(s8[14680064]{0:T(1024)(128)(4,1)} %bitcast.44), calls=%async_computation.5 | async-start | bytes 8388608
  102.6 8.2 %slice-start.3 = ((s8[14680064]{0:T(1024)(128)(4,1)}), s8[2097152]{0:T(1024)(128)(4,1)S(1)}, s32[]{:S(2)}) async-start(s8[14680064]{0:T(1024)(128)(4,1)} %bitcast.44), calls=%async_computation.6 | async-start | bytes 4194304
  147.7 6.6 %copy-start = (f32[16,8]{0,1:T(8,128)S(1)}, f32[16,8]{0,1:T(8,128)}, u32[]{:S(2)}) copy-start(f32[16,8]{0,1:T(8,128)} %param.8) | copy-start | bytes 1540
  147.7 48.3 %all-to-all-start.1 = ((bf16[16,16,3584]{2,1,0:T(8,128)(2,1)}), bf16[16,16,3584]{2,1,0:T(8,128)(2,1)S(1)}, u32[]{:S(2)}, u32[]{:S(2)}) async-start(bf16[16,16,3584]{2,1,0:T(8,128)(2,1)} %bitcast.42), calls=%async_computation.1 | async-start | bytes 3670016 | tf_op jit(solution)/shard_map/all_to_all | solution.py:47
Sparse Core Ops, SparseCore 0:
  115.8 21.1 all-gather.1
where the time goes:
time: 205 us
  blocking collectives  93.4 us (46%)
  waiting for transfers between devices  62.9 us (31%)
  matrix products  24.4 us (12%)
  between operations  13.5 us (7%)
  starting transfers between devices  6.51 us (3%)
  local copies, waits for them, and re-layouts  3.69 us (2%)
    all_to_all x1, blocking collectives, per_device(): lax.all_to_all(outbound, 'ep', split_axis=0, concat_axis=0, tiled=True)  88.5 us
    all_to_all x1, waiting for transfers between devices, per_device(): lax.all_to_all(result, 'ep', split_axis=0, concat_axis=0, tiled=True)  41.6 us
    all_gather x1, waiting for transfers between devices, per_device(): lax.all_gather(hidden, 'tp', axis=1, tiled=True)  21.3 us
    dot_general x1, matrix products, per_device(): jnp.dot(lax.all_gather(hidden, 'tp', axis=1, tiled=True), down_local, pre...  10.7 us
    dot_general x1, matrix products, per_device(): gate_sum = jnp.dot(in_rows, gate_local, preferred_element_type=jnp.float32)  7.39 us
    all_to_all x1, starting transfers between devices, per_device(): lax.all_to_all(result, 'ep', split_axis=0, concat_axis=0, tiled=True)  6.5 us
    all_gather x1, blocking collectives, per_device(): source = lax.all_gather(tokens, 'tp', axis=1, tiled=True)  4.9 us
    dot_general x1, matrix products, per_device(): up_sum = jnp.dot(in_rows, up_local, preferred_element_type=jnp.float32)  4.82 us
  transfers between devices with their start and end apart: 2, of which 2 were waited for; matrix products, arithmetic and copies ran while one was open for 0% of the time, Pallas kernels for 0%

commit v1 on v0

v1 whole, which is shorter than its diff:
```python
import jax
import jax.numpy as jnp
from jax import lax
from jax.sharding import PartitionSpec as P


def per_device(tokens, expert_ids, gate_weights, w_gate, w_up, w_down):
    n_experts = lax.axis_size("ep")
    experts = jnp.arange(n_experts, dtype=jnp.int32)
    chosen = expert_ids[:, :, None] == experts[None, None, :]
    share = jnp.sum(jnp.where(chosen, gate_weights[:, :, None], 0.0), axis=1)
    share = lax.all_gather(share, "ep", axis=0, tiled=True)
    mine = experts == lax.axis_index("ep")
    share = jnp.sum(jnp.where(mine[None, :], share, 0.0), axis=1, keepdims=True)
    rows = lax.all_gather(tokens, "tp", axis=1, tiled=True)
    rows = lax.all_gather(rows, "ep", axis=0, tiled=True)
    gate_sum = jnp.dot(rows, w_gate[0], preferred_element_type=jnp.float32)
    up_sum = jnp.dot(rows, w_up[0], preferred_element_type=jnp.float32)
    hidden = (jax.nn.silu(gate_sum) * up_sum).astype(jnp.bfloat16)
    hidden = lax.all_gather(hidden, "tp", axis=1, tiled=True)
    result = jnp.dot(hidden, w_down[0], preferred_element_type=jnp.float32)
    result = (result * share).astype(jnp.bfloat16)
    return lax.psum_scatter(result, "ep", scatter_dimension=0, tiled=True)


def solution(mesh):
    return jax.shard_map(
        per_device,
        mesh=mesh,
        in_specs=(
            P("ep", "tp"),
            P("ep", None),
            P("ep", None),
            P("ep", None, "tp"),
            P("ep", None, "tp"),
            P("ep", None, "tp"),
        ),
        out_specs=P("ep", "tp"),
        check_vma=False,
    )
```

time: 205 us -> 180 us (0.88)
  the two profiles are of different devices: /device:TPU:11 before, /device:TPU:0 now
where the time goes in v1:
time: 180 us
  waiting for transfers between devices  109 us (61%)
  matrix products  29.4 us (16%)
  blocking collectives  28.4 us (16%)
  between operations  13.2 us (7%)
    reduce_scatter x1, waiting for transfers between devices, per_device(): return lax.psum_scatter(result, 'ep', scatter_dimension=0, tiled=True)  60.6 us
    all_gather x1, waiting for transfers between devices, per_device(): rows = lax.all_gather(rows, 'ep', axis=0, tiled=True)  47.9 us
    all_gather x1, blocking collectives, per_device(): share = lax.all_gather(share, 'ep', axis=0, tiled=True)  19.8 us
    dot_general x1, matrix products, per_device(): result = jnp.dot(hidden, w_down[0], preferred_element_type=jnp.float32)  10.7 us
    dot_general x1, matrix products, per_device(): gate_sum = jnp.dot(rows, w_gate[0], preferred_element_type=jnp.float32)  10.2 us
    all_gather x1, blocking collectives, per_device(): rows = lax.all_gather(tokens, 'tp', axis=1, tiled=True)  8.61 us
    dot_general x1, matrix products, per_device(): up_sum = jnp.dot(rows, w_up[0], preferred_element_type=jnp.float32)  8.41 us
  transfers between devices with their start and end apart: 3, of which 3 were waited for; matrix products, arithmetic and copies ran while one was open for 0% of the time, Pallas kernels for 0%

profile of v1, /device:TPU:0, one launch (start us, length us, event | category | flops | bytes accessed | tf_op | source)
XLA Modules:
  0.0 180.3 jit_solution(2536256150789129163)
XLA Ops:
  6.5 0.0 all-gather.3.cloned.1.call-start
  6.5 8.6 %all_gather.12 = bf16[16,7168]{1,0:T(8,128)(2,1)} all-gather(bf16[16,3584]{1,0:T(8,128)(2,1)} %param.6), channel_id=1, replica_groups=mesh['ep'=16,'tp'=2] {'tp'}, dimensions={1}, use_global_device_ids=true | all-gather | bytes 344064 | tf_op jit(solution)/shard_map/all_gather | solution.py:15
  15.1 0.0 all-gather.3.cloned.1.call-update
  15.2 0.0 all-gather.5.cloned.1.call-start
  15.2 47.9 %all-gather.3.cloned.1.call-done = bf16[256,7168]{1,0:T(8,128)(2,1)} async-done(((bf16[16,7168]{1,0:T(8,128)(2,1)}), bf16[256,7168]{1,0:T(8,128)(2,1)}) %all-gather.3.cloned.1.call-update) | async-done | bytes 3670032 | tf_op jit(solution)/shard_map/all_gather | solution.py:16
  63.1 0.0 copy-start.2
  63.1 10.2 %fusion.4 = f32[256,1024]{1,0:T(8,128)S(1)} fusion(bf16[256,7168]{1,0:T(8,128)(2,1)} %all-gather.3.cloned.1.call-done, bf16[1,7168,1024]{2,1,0:T(8,128)(2,1)} %param.9), kind=kOutput, calls=%fused_computation.4 | convolution fusion | flops 3758096384 | bytes 19398656 | tf_op jit(solution)/shard_map/dot_general | solution.py:17
  73.4 0.0 copy-done.2
  73.4 0.0 copy-start
  73.4 0.0 copy-start.1
  73.4 8.4 %fusion.15 = bf16[256,1024]{1,0:T(8,128)(2,1)} fusion(bf16[256,7168]{1,0:T(8,128)(2,1)S(1)} %copy-done.2, bf16[1,7168,1024]{2,1,0:T(8,128)(2,1)} %param.10, f32[256,1024]{1,0:T(8,128)S(1)} %fusion.4), kind=kOutput, calls=%fused_computation.9 | convolution fusion | flops 3759669248 | bytes 19922944 | tf_op jit(solution)/shard_map/dot_general | solution.py:18
  81.8 0.0 all-gather.5.cloned.1.call-update
  81.8 0.0 reduce-scatter.2.cloned.1.call-start
  81.9 0.0 copy-done
  81.9 0.1 copy.10
  82.0 0.0 copy-done.1
  82.0 0.1 copy.9
  82.1 0.1 select_reduce_fusion.1
  82.2 19.8 %all_gather.15 = f32[256,16]{1,0:T(8,128)S(1)} all-gather(f32[16,16]{1,0:T(8,128)S(1)} %select_reduce_fusion.1), channel_id=1, replica_groups=mesh['ep'=16,'tp'=2] {'ep'}, dimensions={0}, use_global_device_ids=true | all-gather | bytes 17408 | tf_op jit(solution)/shard_map/all_gather | solution.py:12
  102.0 0.1 select_reduce_fusion
  102.1 0.3 all-gather.5.cloned.1.call-done
  102.4 10.7 %fusion.9 = bf16[256,3584]{1,0:T(8,128)(2,1)} fusion(bf16[256,2048]{1,0:T(8,128)(2,1)} %all-gather.5.cloned.1.call-done, bf16[1,2048,3584]{2,1,0:T(8,128)(2,1)} %param.11, f32[256]{0:T(256)S(1)} %select_reduce_fusion), kind=kOutput, calls=%fused_computation.7 | convolution fusion | flops 3759931392 | bytes 17564672 | tf_op jit(solution)/shard_map/dot_general | solution.py:21
  113.1 0.0 reduce-scatter.2.cloned.1.call-update
  113.1 60.6 %reduce-scatter.2.cloned.1.call-done = bf16[16,3584]{1,0:T(8,128)(2,1)} async-done(((bf16[256,3584]{1,0:T(8,128)(2,1)}), bf16[16,3584]{1,0:T(8,128)(2,1)}) %reduce-scatter.2.cloned.1.call-update) | async-done | bytes 114704 | tf_op jit(solution)/shard_map/reduce_scatter | solution.py:23
  (1 shorter events, 0.0 us)
Async XLA Ops:
  6.5 56.6 %all-gather.3.cloned.1.call-start = ((), (), s32[]{:S(2)}) async-start(), calls=%async_computation.1 | async-start | bytes 3899392 | tf_op jit(solution)/shard_map/all_gather | solution.py:16
  15.2 87.2 %all-gather.5.cloned.1.call-start = ((), (), s32[]{:S(2)}) async-start(), calls=%async_computation.2 | async-start | bytes 1572864 | tf_op jit(solution)/shard_map/all_gather | solution.py:20
  63.1 10.3 %copy-start.2 = (bf16[256,7168]{1,0:T(8,128)(2,1)S(1)}, bf16[256,7168]{1,0:T(8,128)(2,1)}, u32[]{:S(2)}) copy-start(bf16[256,7168]{1,0:T(8,128)(2,1)} %all-gather.3.cloned.1.call-done) | copy-start | bytes 11010052
  73.4 8.5 %copy-start = (f32[16,8]{0,1:T(8,128)S(1)}, f32[16,8]{0,1:T(8,128)}, u32[]{:S(2)}) copy-start(f32[16,8]{0,1:T(8,128)} %param.8) | copy-start | bytes 1540
  73.4 8.6 %copy-start.1 = (s32[16,8]{0,1:T(8,128)S(1)}, s32[16,8]{0,1:T(8,128)}, u32[]{:S(2)}) copy-start(s32[16,8]{0,1:T(8,128)} %param.7) | copy-start | bytes 1540
  81.8 91.9 %reduce-scatter.2.cloned.1.call-start = ((), (), s32[]{:S(2)}) async-start(), calls=%async_computation.3 | async-start | bytes 1949696 | tf_op jit(solution)/shard_map/reduce_scatter | solution.py:23
Sparse Core Ops, SparseCore 0:
  15.3 47.7 all-gather.2
  82.0 20.3 all-gather.4
  113.2 60.4 reduce-scatter.1

commit v2 on v1

--- a/solution.py
+++ b/solution.py
@@ -1,16 +1,27 @@
+import functools
+
 import jax
 import jax.numpy as jnp
 from jax import lax
+from jax.experimental import pallas as pl
+from jax.experimental.pallas import tpu as pltpu
 from jax.sharding import PartitionSpec as P
 
-
-def per_device(tokens, expert_ids, gate_weights, w_gate, w_up, w_down):
-    n_experts = lax.axis_size("ep")
+MESH = pl.DeviceIdType.MESH
+LANES = 128
+
+
+def share_of(expert_ids, gate_weights, n_experts):
     experts = jnp.arange(n_experts, dtype=jnp.int32)
     chosen = expert_ids[:, :, None] == experts[None, None, :]
-    share = jnp.sum(jnp.where(chosen, gate_weights[:, :, None], 0.0), axis=1)
+    return jnp.sum(jnp.where(chosen, gate_weights[:, :, None], 0.0), axis=1)
+
+
+def plain(tokens, expert_ids, gate_weights, w_gate, w_up, w_down):
+    n_experts = lax.axis_size("ep")
+    share = share_of(expert_ids, gate_weights, n_experts)
     share = lax.all_gather(share, "ep", axis=0, tiled=True)
-    mine = experts == lax.axis_index("ep")
+    mine = jnp.arange(n_experts, dtype=jnp.int32) == lax.axis_index("ep")
     share = jnp.sum(jnp.where(mine[None, :], share, 0.0), axis=1, keepdims=True)
     rows = lax.all_gather(tokens, "tp", axis=1, tiled=True)
     rows = lax.all_gather(rows, "ep", axis=0, tiled=True)
@@ -23,9 +34,268 @@
     return lax.psum_scatter(result, "ep", scatter_dimension=0, tiled=True)
 
 
+def kernel(tok, shares, wg_hbm, wu_hbm, wd_hbm, out,
+           x_buf, wg, wu, wd, hid, acc, part, r0, s0, r1, s1, r2, sh, col,
+           w_sem, own_sem, own_s, own_r, sh_s, sh_r, z_s, z_r, s_s, s_r, t_s, t_r, b_s, b_r,
+           h_s, h_r, q0_s, q0_r, q1_s, q1_r, q2_s, q2_r):
+    e = lax.axis_index("ep")
+    y = lax.axis_index("tp")
+    z, x, c = e // 4, (e // 2) % 2, e % 2
+    zh, zl = z // 2, z % 2
+    wide = tok.shape[1] // 2
+    n_q = part.shape[0]
+    q_cols = part.shape[3]
+
+    def at(z_, x_, c_, y_):
+        return ((z_ * 2 + x_) * 2 + c_, y_)
+
+    z_of = [z, zh * 2 + 1 - zl, (1 - zh) * 2 + zl, (1 - zh) * 2 + 1 - zl]
+    sib = at(z, x, 1 - c, y)
+    x_peer = at(z, 1 - x, c, y)
+    y_peer = (e, 1 - y)
+    sx, sy = x + (1 - c) * (1 - 2 * x), y + c * (1 - 2 * y)
+    tx, ty = x + c * (1 - 2 * x), y + (1 - c) * (1 - 2 * y)
+    s_peer, t_peer = at(z, sx, c, sy), at(z, tx, c, ty)
+
+    def block(z_, x_, y_, c_):
+        return x_buf.at[2 * y_ + c_, :, pl.ds(16 * (4 * x_ + z_), 16), :]
+
+    def own_block(color, c_):
+        return x_buf.at[2 * y + color, c_, pl.ds(16 * (4 * x + z), 16), :]
+
+    def remote(src, dst, ss, rs, dev):
+        return pltpu.make_async_remote_copy(
+            src_ref=src, dst_ref=dst, send_sem=ss, recv_sem=rs, device_id=dev, device_id_type=MESH
+        )
+
+    loads = []
+    for k in range(4):
+        kb = pl.ds(k * wide, wide)
+        loads.append(pltpu.make_async_copy(wg_hbm.at[0, kb, :], wg.at[k], w_sem.at[2 * k]))
+        loads.append(pltpu.make_async_copy(wu_hbm.at[0, kb, :], wu.at[k], w_sem.at[2 * k + 1]))
+    half = wd.shape[1]
+    for k in range(2):
+        loads.append(
+            pltpu.make_async_copy(wd_hbm.at[0, pl.ds(k * half, half), :], wd.at[k], w_sem.at[8 + k])
+        )
+
+    barrier = pltpu.get_barrier_semaphore()
+    for i in range(1, 16):
+        pl.semaphore_signal(barrier, inc=1, device_id=((e + i) % 16, y), device_id_type=MESH)
+    pl.semaphore_signal(barrier, inc=1, device_id=y_peer, device_id_type=MESH)
+    own = [
+        pltpu.make_async_copy(tok.at[:, pl.ds(k * wide, wide)], own_block(k, c), own_sem.at[k])
+        for k in range(2)
+    ]
+    for cp in own:
+        cp.start()
+    for cp in loads:
+        cp.start()
+    pl.semaphore_wait(barrier, 16)
+
+    sent = []
+
+    def go(src, dst, ss, rs, dev):
+        cp = remote(src, dst, ss, rs, dev)
+        cp.start()
+        sent.append(cp)
+
+    for k in range(2):
+        go(tok.at[:, pl.ds(k * wide, wide)], own_block(k, c), own_s.at[k], own_r.at[k], sib)
+
+    own[0].wait()
+    own[1].wait()
+    for k in range(2):
+        remote(own_block(k, 1 - c), own_block(k, 1 - c), own_s.at[k], own_r.at[k], sib).wait_recv()
+
+    def same(ref, ss, rs, dev):
+        go(ref, ref, ss, rs, dev)
+
+    def got(ref, rs):
+        remote(ref, ref, own_s.at[0], rs, sib).wait_recv()
+
+    mine = block(z, x, y, c)
+    same(mine, s_s.at[0], s_r.at[0], s_peer)
+    same(mine, t_s.at[0], t_r.at[0], t_peer)
+    for k in range(1, 4):
+        same(mine, z_s.at[k - 1], z_r.at[k - 1], at(z_of[k], x, c, y))
+
+    pos = (c * 2 + x) * 4 + z
+    for i in range(1, 16):
+        to = (e + i) % 16
+        go(shares.at[to], sh.at[pos], sh_s.at[i - 1], sh_r.at[i - 1], (to, y))
+    own_share = pltpu.make_async_copy(shares.at[e], sh.at[pos], own_sem.at[2])
+    own_share.start()
+
+    for k in range(1, 4):
+        b = block(z_of[k], x, y, c)
+        got(b, z_r.at[k - 1])
+        same(b, s_s.at[k], s_r.at[k], s_peer)
+        same(b, t_s.at[k], t_r.at[k], t_peer)
+        same(b, b_s.at[k - 1], b_r.at[k - 1], sib)
+    for k in range(4):
+        b = block(z_of[k], sx, sy, c)
+        got(b, s_r.at[k])
+        same(b, t_s.at[4 + k], t_r.at[4 + k], t_peer)
+        same(b, b_s.at[3 + k], b_r.at[3 + k], sib)
+    for f in range(2):
+        for k in range(4):
+            fx = tx if f == 0 else 1 - x
+            fy = ty if f == 0 else 1 - y
+            b = block(z_of[k], fx, fy, c)
+            got(b, t_r.at[4 * f + k])
+            same(b, b_s.at[7 + 4 * f + k], b_r.at[7 + 4 * f + k], sib)
+
+    own_share.wait()
+    for i in range(1, 16):
+        remote(sh.at[pos], sh.at[pos], sh_s.at[i - 1], sh_r.at[i - 1], sib).wait_recv()
+    pick = lax.broadcasted_iota(jnp.int32, (16, LANES), 0) == lax.broadcasted_iota(
+        jnp.int32, (16, LANES), 1
+    )
+    for p in range(16):
+        row = jnp.where(pick, sh[p], 0.0)
+        col[pl.ds(16 * p, 16), :] = jnp.sum(row, axis=1, keepdims=True)
+
+    for i in range(15):
+        got(mine, b_r.at[i])
+    for cp in loads[:8]:
+        cp.wait()
+
+    rows = 256
+    n_h = h_s.shape[0]
+    h_cols = hid.shape[2] // n_h
+
+    def hidden_copy(n):
+        ref = hid.at[y, :, pl.ds(pl.multiple_of(n * h_cols, h_cols), h_cols)]
+        return remote(ref, ref, h_s.at[n], h_r.at[n], y_peer)
+
+    @pl.loop(0, n_h)
+    def _(n):
+        cols = pl.ds(pl.multiple_of(n * h_cols, h_cols), h_cols)
+        g = jnp.zeros((rows, h_cols), jnp.float32)
+        u = jnp.zeros((rows, h_cols), jnp.float32)
+        for k in range(4):
+            xk = x_buf[k].reshape(rows, wide)
+            g = g + jnp.dot(xk, wg[k, :, cols], preferred_element_type=jnp.float32)
+            u = u + jnp.dot(xk, wu[k, :, cols], preferred_element_type=jnp.float32)
+        hid[y, :, cols] = (g / (1.0 + jnp.exp(-g)) * u).astype(jnp.bfloat16)
+        hidden_copy(n).start()
+
+    for cp in loads[8:]:
+        cp.wait()
+
+    @pl.loop(0, n_q)
+    def _(q):
+        cols = pl.ds(pl.multiple_of(q * q_cols, q_cols), q_cols)
+        acc[:, cols] = jnp.dot(hid[y], wd[y, :, cols], preferred_element_type=jnp.float32)
+
+    for n in range(n_h):
+        hidden_copy(n).wait()
+
+    def r0_copy(q):
+        return remote(part.at[q, 1 - c], r0.at[q], q0_s.at[q], q0_r.at[q], sib)
+
+    def r1_copy(q):
+        src = s0.at[q, pl.ds(64 * (1 - x), 64), :]
+        return remote(src, r1.at[q], q1_s.at[q], q1_r.at[q], x_peer)
+
+    def r2_copy(q, k):
+        src = s1.at[q, pl.ds(16 * z_of[k], 16), :]
+        return remote(
+            src, r2.at[q, k - 1], q2_s.at[3 * q + k - 1], q2_r.at[3 * q + k - 1], at(z_of[k], x, c, y)
+        )
+
+    f32 = jnp.float32
+
+    @pl.loop(0, n_q + 3)
+    def _(i):
+        @pl.when(i < n_q)
+        def _():
+            cols = pl.ds(pl.multiple_of(i * q_cols, q_cols), q_cols)
+            r = acc[:, cols] + jnp.dot(hid[1 - y], wd[1 - y, :, cols], preferred_element_type=f32)
+            part[i] = (r * col[...]).astype(jnp.bfloat16).reshape(2, rows // 2, q_cols)
+            r0_copy(i).start()
+
+        @pl.when((i >= 1) & (i < n_q + 1))
+        def _():
+            q = i - 1
+            r0_copy(q).wait()
+            s0[q] = (part[q, c].astype(f32) + r0[q].astype(f32)).astype(jnp.bfloat16)
+            r1_copy(q).start()
+
+        @pl.when((i >= 2) & (i < n_q + 2))
+        def _():
+            q = i - 2
+            r1_copy(q).wait()
+            keep = s0[q, pl.ds(pl.multiple_of(64 * x, 64), 64), :].astype(f32)
+            s1[q] = (keep + r1[q].astype(f32)).astype(jnp.bfloat16)
+            for k in range(1, 4):
+                r2_copy(q, k).start()
+
+        @pl.when(i >= 3)
+        def _():
+            q = i - 3
+            total = s1[q, pl.ds(pl.multiple_of(16 * z, 16), 16), :].astype(f32)
+            for k in range(1, 4):
+                r2_copy(q, k).wait()
+                total = total + r2[q, k - 1].astype(f32)
+            out[:, pl.ds(pl.multiple_of(q * q_cols, q_cols), q_cols)] = total.astype(jnp.bfloat16)
+
+    for cp in sent:
+        cp.wait_send()
+
+
+def fused(tokens, expert_ids, gate_weights, w_gate, w_up, w_down):
+    bf16, f32 = jnp.bfloat16, jnp.float32
+    width = tokens.shape[1]
+    depth, units = w_gate.shape[1], w_gate.shape[2]
+    share = share_of(expert_ids, gate_weights, 16).T
+    share = jnp.pad(share, ((0, 0), (0, LANES - 16)))[:, None, :]
+    n_q, n_h = 7, 4
+    q_cols = width // n_q
+    wide = width // 2
+    vmem, dma = pltpu.VMEM, pltpu.SemaphoreType.DMA
+    hbm = pl.BlockSpec(memory_space=pl.ANY)
+    return pl.pallas_call(
+        kernel,
+        out_shape=jax.ShapeDtypeStruct((16, width), bf16),
+        in_specs=[hbm] * 5,
+        out_specs=pl.BlockSpec(memory_space=pltpu.VMEM),
+        scratch_shapes=[
+            vmem((4, 2, 128, wide), bf16),
+            vmem((4, wide, units), bf16),
+            vmem((4, wide, units), bf16),
+            vmem((2, units, width), bf16),
+            vmem((2, 256, units), bf16),
+            vmem((256, width), f32),
+            vmem((n_q, 2, 128, q_cols), bf16),
+            vmem((n_q, 128, q_cols), bf16),
+            vmem((n_q, 128, q_cols), bf16),
+            vmem((n_q, 64, q_cols), bf16),
+            vmem((n_q, 64, q_cols), bf16),
+            vmem((n_q, 3, 16, q_cols), bf16),
+            vmem((16, 1, LANES), f32),
+            vmem((256, 1), f32),
+            dma((10,)), dma((3,)), dma((2,)), dma((2,)), dma((15,)), dma((15,)),
+            dma((3,)), dma((3,)), dma((4,)), dma((4,)), dma((8,)), dma((8,)), dma((15,)), dma((15,)),
+            dma((n_h,)), dma((n_h,)),
+            dma((n_q,)), dma((n_q,)), dma((n_q,)), dma((n_q,)), dma((3 * n_q,)), dma((3 * n_q,)),
+        ],
+        compiler_params=pltpu.CompilerParams(
+            collective_id=0, has_side_effects=True, vmem_limit_bytes=62_000_000
+        ),
+        cost_estimate=pl.CostEstimate(
+            flops=2 * 256 * (depth * units * 2 + 2 * units * width),
+            bytes_accessed=2 * (2 * depth * units + 2 * units * width),
+            transcendentals=256 * units,
+        ),
+    )(tokens, share, w_gate, w_up, w_down)
+
+
 def solution(mesh):
+    one_kernel = mesh.shape["ep"] == 16 and mesh.shape["tp"] == 2
     return jax.shard_map(
-        per_device,
+        fused if one_kernel else plain,
         mesh=mesh,
         in_specs=(
             P("ep", "tp"),

time: 180 us -> 83.1 us (0.46)
  waiting for transfers between devices: 109 us -> 0 us
  Pallas kernels: 0 us -> 79 us
  matrix products: 29.4 us -> 0 us
  blocking collectives: 28.4 us -> 0 us
  between operations: 13.2 us -> 0.02 us
  local copies, waits for them, and re-layouts: 0.16 us -> 3.74 us
    pallas_call x0 -> x1, Pallas kernels: none -> 79 us  [fused(): pl.pallas_call(kernel, out_shape=jax.ShapeDtypeStruct((16, width), bf16),...]
    reduce_scatter x1 -> x0, waiting for transfers between devices: 60.6 us -> none  [per_device(): return lax.psum_scatter(result, 'ep', scatter_dimension=0, tiled=True)]
    all_gather x2 -> x0, waiting for transfers between devices: 48.2 us -> none  [the longest x1 47.9 us: per_device(): rows = lax.all_gather(rows, 'ep', axis=0, tiled=True)]
    dot_general x3 -> x0, matrix products: 29.4 us -> none  [the longest x1 10.7 us: per_device(): result = jnp.dot(hidden, w_down[0], preferred_element_type=jnp.float32)]
    all_gather x2 -> x0, blocking collectives: 28.4 us -> none  [the longest x1 19.8 us: per_device(): share = lax.all_gather(share, 'ep', axis=0, tiled=True)]
    unnamed x8 -> x3, local copies, waits for them, and re-layouts: 0.16 us -> 3.07 us
  transfers between devices with their start and end apart: 3 -> 0, of which waited for: 3 -> 0; matrix products, arithmetic and copies ran while one was open for 0% -> 0% of each run, Pallas kernels for 0% -> 0%
where the time goes in v2:
time: 83.1 us; the launch traced here: 82.9 us
  Pallas kernels  79 us (95%)
  local copies, waits for them, and re-layouts  3.74 us (5%)
    pallas_call x1, Pallas kernels, fused(): pl.pallas_call(kernel, out_shape=jax.ShapeDtypeStruct((16, width), bf16),...  79 us
    unnamed x3, local copies, waits for them, and re-layouts  3.07 us

profile of v2, /device:TPU:0, one launch (start us, length us, event | category | flops | bytes accessed | tf_op | source)
XLA Modules:
  0.0 82.9 jit_solution(4748138979134096706)
XLA Ops:
  0.0 0.8 copy.9
  0.8 0.8 copy.10
  1.5 0.1 select_reduce_fusion
  1.6 0.1 copy.11
  1.7 0.6 pad.4
  2.3 79.0 %shard_map.64 = bf16[16,3584]{1,0:T(8,128)(2,1)} custom-call(bf16[16,3584]{1,0:T(8,128)(2,1)} %tok.1, f32[16,1,128]{2,1,0:T(1,128)} %bitcast.3, bf16[1,7168,1024]{2,1,0:T(8,128)(2,1)} %wg_hbm.1, bf16[1,7168,1024]{2,1,0:T(8,128)(2,1)} %wu_hbm.1, bf16[1,2048,3584]{2,1,0:T(8,128)(2,1)} %wd_hbm.1), custom_call_target="tpu_custom_call" | custom-call | flops 11274289152 | bytes 44040192 | tf_op jit(solution)/shard_map/pallas_call | solution.py:259
  81.4 1.6 %copy.13 = bf16[16,3584]{1,0:T(8,128)(2,1)} copy(bf16[16,3584]{1,0:T(8,128)(2,1)} %shard_map.64) | data formatting | bytes 229376

commit v3 on v2

--- a/solution.py
+++ b/solution.py
@@ -36,7 +36,7 @@
 
 def kernel(tok, shares, wg_hbm, wu_hbm, wd_hbm, out,
            x_buf, wg, wu, wd, hid, acc, part, r0, s0, r1, s1, r2, sh, col,
-           w_sem, own_sem, own_s, own_r, sh_s, sh_r, z_s, z_r, s_s, s_r, t_s, t_r, b_s, b_r,
+           w_sem, own_sem, own_s, own_r, sh_s, sh_r, zu_s, zu_r, zd_s, zd_r, s_s, s_r, t_s, t_r, b_s, b_r,
            h_s, h_r, q0_s, q0_r, q1_s, q1_r, q2_s, q2_r):
     e = lax.axis_index("ep")
     y = lax.axis_index("tp")
@@ -89,8 +89,6 @@
     ]
     for cp in own:
         cp.start()
-    for cp in loads:
-        cp.start()
     pl.semaphore_wait(barrier, 16)
 
     sent = []
@@ -115,10 +113,28 @@
         remote(ref, ref, own_s.at[0], rs, sib).wait_recv()
 
     mine = block(z, x, y, c)
-    same(mine, s_s.at[0], s_r.at[0], s_peer)
-    same(mine, t_s.at[0], t_r.at[0], t_peer)
-    for k in range(1, 4):
-        same(mine, z_s.at[k - 1], z_r.at[k - 1], at(z_of[k], x, c, y))
+
+    def up(d):
+        b = block(z - d + 1, x, y, c)
+        return remote(b, b, zu_s.at[d - 1], zu_r.at[d - 1], at(z + 1, x, c, y))
+
+    def down(d):
+        b = block(z + d - 1, x, y, c)
+        return remote(b, b, zd_s.at[d - 1], zd_r.at[d - 1], at(z - 1, x, c, y))
+
+    def up_goes(d):
+        return (z < 3) & (z >= d - 1)
+
+    def down_goes(d):
+        return (z > 0) & (z <= 4 - d)
+
+    def pair(ref, ss, rs, i, dev):
+        return remote(ref, ref, ss.at[i], rs.at[i], dev)
+
+    pl.when(up_goes(1))(lambda: up(1).start())
+    pl.when(down_goes(1))(lambda: down(1).start())
+    pair(mine, t_s, t_r, z, t_peer).start()
+    pair(mine, s_s, s_r, z, s_peer).start()
 
     pos = (c * 2 + x) * 4 + z
     for i in range(1, 16):
@@ -126,25 +142,51 @@
         go(shares.at[to], sh.at[pos], sh_s.at[i - 1], sh_r.at[i - 1], (to, y))
     own_share = pltpu.make_async_copy(shares.at[e], sh.at[pos], own_sem.at[2])
     own_share.start()
-
-    for k in range(1, 4):
-        b = block(z_of[k], x, y, c)
-        got(b, z_r.at[k - 1])
-        same(b, s_s.at[k], s_r.at[k], s_peer)
-        same(b, t_s.at[k], t_r.at[k], t_peer)
-        same(b, b_s.at[k - 1], b_r.at[k - 1], sib)
-    for k in range(4):
-        b = block(z_of[k], sx, sy, c)
-        got(b, s_r.at[k])
-        same(b, t_s.at[4 + k], t_r.at[4 + k], t_peer)
-        same(b, b_s.at[3 + k], b_r.at[3 + k], sib)
-    for f in range(2):
-        for k in range(4):
-            fx = tx if f == 0 else 1 - x
-            fy = ty if f == 0 else 1 - y
-            b = block(z_of[k], fx, fy, c)
-            got(b, t_r.at[4 * f + k])
-            same(b, b_s.at[7 + 4 * f + k], b_r.at[7 + 4 * f + k], sib)
+    for cp in loads:
+        cp.start()
+
+    def landed(zp, moving, d, coming):
+        b = block(zp, x, y, c)
+        got(b, coming.at[d - 1])
+        if d < 3:
+            goes = up_goes(d + 1) if moving == "up" else down_goes(d + 1)
+            pl.when(goes)(lambda: (up if moving == "up" else down)(d + 1).start())
+        pair(b, s_s, s_r, zp, s_peer).start()
+        pair(b, t_s, t_r, zp, t_peer).start()
+        pair(b, b_s, b_r, zp, sib).start()
+
+    def landed_s(zp):
+        b = block(zp, sx, sy, c)
+        got(b, s_r.at[zp])
+        pair(b, t_s, t_r, 4 + zp, t_peer).start()
+        pair(b, b_s, b_r, 4 + zp, sib).start()
+
+    def landed_t(zp):
+        b = block(zp, tx, ty, c)
+        got(b, t_r.at[zp])
+        pair(b, b_s, b_r, 8 + zp, sib).start()
+
+    for d in range(1, 4):
+        pl.when(z >= d)(lambda d=d: landed(z - d, "up", d, zu_r))
+        pl.when(z + d <= 3)(lambda d=d: landed(z + d, "down", d, zd_r))
+        if d == 1:
+            landed_s(z)
+            landed_t(z)
+        else:
+            for f in (landed_s, landed_t):
+                pl.when(z >= d - 1)(lambda d=d, f=f: f(z - d + 1))
+                pl.when(z + d - 1 <= 3)(lambda d=d, f=f: f(z + d - 1))
+    for f in (landed_s, landed_t):
+        pl.when(z >= 3)(lambda f=f: f(z - 3))
+        pl.when(z <= 0)(lambda f=f: f(z + 3))
+    for d in range(4):
+        def landed_ts(zp):
+            b = block(zp, 1 - x, 1 - y, c)
+            got(b, t_r.at[4 + zp])
+            pair(b, b_s, b_r, 12 + zp, sib).start()
+        pl.when(z >= d)(lambda d=d, f=landed_ts: f(z - d))
+        if d:
+            pl.when(z + d <= 3)(lambda d=d, f=landed_ts: f(z + d))
 
     own_share.wait()
     for i in range(1, 16):
@@ -156,7 +198,9 @@
         row = jnp.where(pick, sh[p], 0.0)
         col[pl.ds(16 * p, 16), :] = jnp.sum(row, axis=1, keepdims=True)
 
-    for i in range(15):
+    for d in range(1, 4):
+        got(mine, b_r.at[z_of[d]])
+    for i in range(4, 16):
         got(mine, b_r.at[i])
     for cp in loads[:8]:
         cp.wait()
@@ -207,7 +251,7 @@
 
     f32 = jnp.float32
 
-    @pl.loop(0, n_q + 3)
+    @pl.loop(0, n_q + 5)
     def _(i):
         @pl.when(i < n_q)
         def _():
@@ -223,24 +267,34 @@
             s0[q] = (part[q, c].astype(f32) + r0[q].astype(f32)).astype(jnp.bfloat16)
             r1_copy(q).start()
 
-        @pl.when((i >= 2) & (i < n_q + 2))
+        @pl.when((i >= 3) & (i < n_q + 3))
         def _():
-            q = i - 2
+            q = i - 3
             r1_copy(q).wait()
             keep = s0[q, pl.ds(pl.multiple_of(64 * x, 64), 64), :].astype(f32)
             s1[q] = (keep + r1[q].astype(f32)).astype(jnp.bfloat16)
             for k in range(1, 4):
                 r2_copy(q, k).start()
 
-        @pl.when(i >= 3)
+        @pl.when(i >= 5)
         def _():
-            q = i - 3
+            q = i - 5
             total = s1[q, pl.ds(pl.multiple_of(16 * z, 16), 16), :].astype(f32)
             for k in range(1, 4):
                 r2_copy(q, k).wait()
                 total = total + r2[q, k - 1].astype(f32)
             out[:, pl.ds(pl.multiple_of(q * q_cols, q_cols), q_cols)] = total.astype(jnp.bfloat16)
 
+    for d in range(1, 4):
+        pl.when(up_goes(d))(lambda d=d: up(d).wait_send())
+        pl.when(down_goes(d))(lambda d=d: down(d).wait_send())
+        pair(mine, b_s, b_r, z_of[d], sib).wait_send()
+    for i in range(4):
+        pair(mine, s_s, s_r, i, s_peer).wait_send()
+    for i in range(8):
+        pair(mine, t_s, t_r, i, t_peer).wait_send()
+    for i in range(4, 16):
+        pair(mine, b_s, b_r, i, sib).wait_send()
     for cp in sent:
         cp.wait_send()
 
@@ -277,7 +331,8 @@
             vmem((16, 1, LANES), f32),
             vmem((256, 1), f32),
             dma((10,)), dma((3,)), dma((2,)), dma((2,)), dma((15,)), dma((15,)),
-            dma((3,)), dma((3,)), dma((4,)), dma((4,)), dma((8,)), dma((8,)), dma((15,)), dma((15,)),
+            dma((3,)), dma((3,)), dma((3,)), dma((3,)), dma((4,)), dma((4,)), dma((8,)), dma((8,)),
+            dma((16,)), dma((16,)),
             dma((n_h,)), dma((n_h,)),
             dma((n_q,)), dma((n_q,)), dma((n_q,)), dma((n_q,)), dma((3 * n_q,)), dma((3 * n_q,)),
         ],

time: 83.1 us -> 68.7 us (0.83)
  Pallas kernels: 79 us -> 64.6 us
    pallas_call x1, Pallas kernels: 79 us -> 64.6 us  [fused(): pl.pallas_call(kernel, out_shape=jax.ShapeDtypeStruct((16, width), bf16),...]
where the time goes in v3:
time: 68.7 us; the launch traced here: 68.4 us
  Pallas kernels  64.6 us (94%)
  local copies, waits for them, and re-layouts  3.74 us (5%)
    pallas_call x1, Pallas kernels, fused(): pl.pallas_call(kernel, out_shape=jax.ShapeDtypeStruct((16, width), bf16),...  64.6 us
    unnamed x3, local copies, waits for them, and re-layouts  3.07 us

profile of v3, /device:TPU:0, one launch (start us, length us, event | category | flops | bytes accessed | tf_op | source)
XLA Modules:
  0.0 68.4 jit_solution(7977091686013959010)
XLA Ops:
  0.0 0.8 %copy.9 = s32[16,8]{1,0:T(8,128)S(1)} copy(s32[16,8]{0,1:T(8,128)} %param.7) | data formatting | bytes 1024 | tf_op args[1]
  0.8 0.8 %copy.10 = f32[16,8]{1,0:T(8,128)S(1)} copy(f32[16,8]{0,1:T(8,128)} %param.8) | data formatting | bytes 1024 | tf_op args[2]
  1.5 0.1 select_reduce_fusion
  1.6 0.1 copy.11
  1.7 0.6 pad.4
  2.3 64.6 %shard_map.64 = bf16[16,3584]{1,0:T(8,128)(2,1)} custom-call(bf16[16,3584]{1,0:T(8,128)(2,1)} %tok.1, f32[16,1,128]{2,1,0:T(1,128)} %bitcast.3, bf16[1,7168,1024]{2,1,0:T(8,128)(2,1)} %wg_hbm.1, bf16[1,7168,1024]{2,1,0:T(8,128)(2,1)} %wu_hbm.1, bf16[1,2048,3584]{2,1,0:T(8,128)(2,1)} %wd_hbm.1), custom_call_target="tpu_custom_call" | custom-call | flops 11274289152 | bytes 44040192 | tf_op jit(solution)/shard_map/pallas_call | solution.py:313
  66.9 1.6 %copy.13 = bf16[16,3584]{1,0:T(8,128)(2,1)} copy(bf16[16,3584]{1,0:T(8,128)(2,1)} %shard_map.64) | data formatting | bytes 229376

commit v4 on v3

--- a/solution.py
+++ b/solution.py
@@ -251,7 +251,7 @@
 
     f32 = jnp.float32
 
-    @pl.loop(0, n_q + 5)
+    @pl.loop(0, n_q + 7)
     def _(i):
         @pl.when(i < n_q)
         def _():
@@ -267,18 +267,18 @@
             s0[q] = (part[q, c].astype(f32) + r0[q].astype(f32)).astype(jnp.bfloat16)
             r1_copy(q).start()
 
-        @pl.when((i >= 3) & (i < n_q + 3))
+        @pl.when((i >= 4) & (i < n_q + 4))
         def _():
-            q = i - 3
+            q = i - 4
             r1_copy(q).wait()
             keep = s0[q, pl.ds(pl.multiple_of(64 * x, 64), 64), :].astype(f32)
             s1[q] = (keep + r1[q].astype(f32)).astype(jnp.bfloat16)
             for k in range(1, 4):
                 r2_copy(q, k).start()
 
-        @pl.when(i >= 5)
+        @pl.when(i >= 7)
         def _():
-            q = i - 5
+            q = i - 7
             total = s1[q, pl.ds(pl.multiple_of(16 * z, 16), 16), :].astype(f32)
             for k in range(1, 4):
                 r2_copy(q, k).wait()

time: 68.7 us -> 67.4 us (0.981)
  Pallas kernels: 64.6 us -> 63.4 us
    pallas_call x1, Pallas kernels: 64.6 us -> 63.4 us  [fused(): pl.pallas_call(kernel, out_shape=jax.ShapeDtypeStruct((16, width), bf16),...]
where the time goes in v4:
time: 67.4 us; the launch traced here: 67.2 us
  Pallas kernels  63.4 us (94%)
  local copies, waits for them, and re-layouts  3.74 us (6%)
    pallas_call x1, Pallas kernels, fused(): pl.pallas_call(kernel, out_shape=jax.ShapeDtypeStruct((16, width), bf16),...  63.4 us
    unnamed x3, local copies, waits for them, and re-layouts  3.07 us

profile of v4, /device:TPU:0, one launch (start us, length us, event | category | flops | bytes accessed | tf_op | source)
XLA Modules:
  0.0 67.2 jit_solution(13002638987872925110)
XLA Ops:
  0.0 0.8 %copy.9 = s32[16,8]{1,0:T(8,128)S(1)} copy(s32[16,8]{0,1:T(8,128)} %param.7) | data formatting | bytes 1024 | tf_op args[1]
  0.8 0.8 %copy.10 = f32[16,8]{1,0:T(8,128)S(1)} copy(f32[16,8]{0,1:T(8,128)} %param.8) | data formatting | bytes 1024 | tf_op args[2]
  1.5 0.1 select_reduce_fusion
  1.6 0.1 copy.11
  1.7 0.6 pad.4
  2.3 63.4 %shard_map.64 = bf16[16,3584]{1,0:T(8,128)(2,1)} custom-call(bf16[16,3584]{1,0:T(8,128)(2,1)} %tok.1, f32[16,1,128]{2,1,0:T(1,128)} %bitcast.3, bf16[1,7168,1024]{2,1,0:T(8,128)(2,1)} %wg_hbm.1, bf16[1,7168,1024]{2,1,0:T(8,128)(2,1)} %wu_hbm.1, bf16[1,2048,3584]{2,1,0:T(8,128)(2,1)} %wd_hbm.1), custom_call_target="tpu_custom_call" | custom-call | flops 11274289152 | bytes 44040192 | tf_op jit(solution)/shard_map/pallas_call | solution.py:313
  65.7 1.6 %copy.13 = bf16[16,3584]{1,0:T(8,128)(2,1)} copy(bf16[16,3584]{1,0:T(8,128)(2,1)} %shard_map.64) | data formatting | bytes 229376
